TPU v7x, 128 devices: a whole 4x4x4 slice. The times are simulated.
128 devices in a mesh: lev: 4 (over y), col: 32 (over x, z, core).
Axes of the slice: x: 4, y: 4, z: 4, core: 2. Of those that a mesh axis runs over, the one named last changes fastest.
Arguments:
- increment: bfloat16 [3, 128, 131072], P(None, 'lev', 'col'), may hold values from -6 to 6
- jacobian: bfloat16 [1024, 616, 384], P(('lev', 'col')), may hold values from -0.3125 to 0.3125
- departure: bfloat16 [616, 1048576], P(None, ('lev', 'col')), may hold values from -6 to 6
- predictor: float32 [8, 1048576], P(None, ('lev', 'col')), may hold values from -5 to 5
- bias_coef: float32 [616, 8], replicated, may hold values from -1.5 to 1.5
- obs_sigma: float32 [616], replicated, may hold values from 0.5 to 2
- channel_use: int32 [1024, 616], P(('lev', 'col')), may hold values 0 or 1
- send_cols: int32 [128, 128, 8], P(('lev', 'col')), may hold values from 0 to 1023
- obs_slot: int32 [1048576], P(('lev', 'col')), may hold values from 0 to 1023, as said below
Outputs:
- gradient: float32 [3, 128, 131072], P(None, 'lev', 'col')
Inputs may be any that keep to these rules, and one draw needn't show every extreme that they name: obs_slot[j] = s * 8 + k; the slots (s, p, k) named by the observations of device p are, for each s, the first few of the 8, at least 2 of them; some device p names all 8 slots of every device.
All inputs are finite; a program needn't handle non-finite values. No bound on the sum of `channel_use` on one device may be relied on, other than what follows from the above.
Results may differ from a plain program's by a relative error of at most 0.001.
Values may be sent and summed in bfloat16 or wider, within the bound.
A program may use at most 128 MiB of HBM per device.

v0:
```python
import jax
import jax.numpy as jnp
from jax import lax
from jax.sharding import PartitionSpec as P


def fetch_rows(outgoing):
    return lax.all_to_all(outgoing, ("lev", "col"), split_axis=0, concat_axis=0, tiled=True)


def return_rows(outgoing):
    return lax.all_to_all(outgoing, ("lev", "col"), split_axis=0, concat_axis=0, tiled=True)


def observe(profile, jacobian, departure, predictor, bias_coef, obs_sigma, channel_use):
    tile_count = jacobian.shape[0]
    channels = jacobian.shape[1]
    obs_count = profile.shape[0]
    profile_len = profile.shape[1]
    obs_tile = obs_count // tile_count
    tangent = jnp.einsum(
        "tcf,tof->cto",
        jacobian,
        profile.reshape(tile_count, obs_tile, profile_len),
        preferred_element_type=jnp.float32,
    )
    bias_term = jnp.dot(
        bias_coef, predictor, precision=lax.Precision.HIGHEST, preferred_element_type=jnp.float32
    )
    residual = tangent - (departure.astype(jnp.float32) - bias_term).reshape(
        channels, tile_count, obs_tile
    )
    inverse_var = 1.0 / (obs_sigma * obs_sigma)
    scaling = channel_use.astype(jnp.float32).T * inverse_var[:, None]
    forcing = (scaling[:, :, None] * residual).astype(jnp.bfloat16)
    return jnp.einsum(
        "tcf,cto->tof", jacobian, forcing, preferred_element_type=jnp.float32
    ).reshape(obs_count, profile_len)


def on_device(
    increment,
    jacobian,
    departure,
    predictor,
    bias_coef,
    obs_sigma,
    channel_use,
    send_cols,
    obs_slot,
):
    lev_size = lax.axis_size("lev")
    col_size = lax.axis_size("col")
    peer_count = lev_size * col_size
    field_count = increment.shape[0]
    capacity = send_cols.shape[2]
    columns = lax.all_to_all(increment, "lev", split_axis=2, concat_axis=1, tiled=True)
    level_count = columns.shape[1]
    column_count = columns.shape[2]
    profile_len = field_count * level_count
    column_rows = columns.reshape(profile_len, column_count).T
    slot_lists = send_cols[0]
    outgoing = column_rows[slot_lists]
    incoming = fetch_rows(outgoing).reshape(peer_count * capacity, profile_len)
    profile = incoming[obs_slot]
    adjoint = observe(profile, jacobian, departure, predictor, bias_coef, obs_sigma, channel_use)
    slot_adjoint = jax.ops.segment_sum(adjoint, obs_slot, num_segments=peer_count * capacity)
    returned = return_rows(slot_adjoint.reshape(peer_count, capacity, profile_len))
    column_adjoint = jax.ops.segment_sum(
        returned.reshape(peer_count * capacity, profile_len),
        slot_lists.reshape(-1),
        num_segments=column_count,
    )
    field_adjoint = column_adjoint.T.reshape(field_count, level_count, column_count)
    return lax.all_to_all(field_adjoint, "lev", split_axis=1, concat_axis=2, tiled=True)


def solution(mesh):
    return jax.shard_map(
        on_device,
        mesh=mesh,
        in_specs=(
            P(None, "lev", "col"),
            P(("lev", "col"), None, None),
            P(None, ("lev", "col")),
            P(None, ("lev", "col")),
            P(),
            P(),
            P(("lev", "col"), None),
            P(("lev", "col"), None, None),
            P(("lev", "col")),
        ),
        out_specs=P(None, "lev", "col"),
        check_vma=False,
    )
```

profile of v0, /device:TPU:1, one launch (start us, length us, event | category | flops | bytes accessed | tf_op | source)
XLA Modules:
  0.0 254.4 jit_solution(5134098283058532032)
XLA Ops:
  0.0 6.0 %copy.31 = bf16[3,32,4096]{1,0,2:T(4,128)(2,1)} copy(bf16[3,32,4096]{2,1,0:T(8,128)(2,1)} %param.9) | data formatting | bytes 1572864 | tf_op args[0]
  6.0 5.6 %reshape.103 = bf16[4,2,49152]{2,1,0:T(2,128)(2,1)} reshape(bf16[4096,3,32]{2,1,0:T(4,128)(2,1)} %bitcast.49) | data formatting | bytes 1572864
  11.6 5.0 %all-to-all-start = ((bf16[4,2,49152]{2,1,0:T(2,128)(2,1)}), bf16[4,2,49152]{2,1,0:T(2,128)(2,1)S(1)}, u32[]{:S(2)}, u32[]{:S(2)}) async-start(bf16[4,2,49152]{2,1,0:T(2,128)(2,1)} %reshape.103), calls=%async_computation | async-start | bytes 1572864 | tf_op jit(solution)/shard_map/all_to_all | solution.py:57
  16.6 0.1 copy.35
  16.7 0.1 reshape.65
  16.9 11.1 %all-to-all-done = bf16[4,2,49152]{2,1,0:T(2,128)(2,1)S(1)} async-done(((bf16[4,2,49152]{2,1,0:T(2,128)(2,1)}), bf16[4,2,49152]{2,1,0:T(2,128)(2,1)S(1)}, u32[]{:S(2)}, u32[]{:S(2)}) %all-to-all-start) | async-done | bytes 786464 | tf_op jit(solution)/shard_map/all_to_all | solution.py:57
  28.0 4.2 %reshape.104 = bf16[4096,3,32]{2,1,0:T(4,128)(2,1)} reshape(bf16[4,2,49152]{2,1,0:T(2,128)(2,1)S(1)} %all-to-all-done) | data formatting | bytes 1572864
  32.2 5.3 %copy.33 = bf16[3,4,32,1024]{3,2,1,0:T(8,128)(2,1)S(1)} copy(bf16[3,4,32,1024]{2,0,3,1:T(4,128)(2,1)} %bitcast.48) | data formatting | bytes 1572864 | tf_op jit(solution)/shard_map/all_to_all | solution.py:57
  37.5 0.4 copy.34
  37.9 5.0 %gather_fusion = bf16[1024,384]{1,0:T(8,128)(2,1)} fusion(bf16[1024,384]{1,0:T(8,128)(2,1)S(1)} %bitcast.46, s32[1024]{0:T(1024)S(1)} %broadcast_clamp_fusion), kind=kCustom, calls=%fused_computation | custom fusion | bytes 1576960 | tf_op jit(solution)/shard_map/gather | solution.py:63
  42.9 9.8 %all-to-all-start.1 = ((bf16[128,8,384]{2,1,0:T(8,128)(2,1)}), bf16[128,8,384]{2,1,0:T(8,128)(2,1)S(1)}, u32[]{:S(2)}, u32[]{:S(2)}) async-start(bf16[128,8,384]{2,1,0:T(8,128)(2,1)} %bitcast.7), calls=%async_computation.1 | async-start | bytes 1572864 | tf_op jit(solution)/shard_map/all_to_all | solution.py:8
  52.8 20.8 %convert_subtract_fusion = f32[616,8192]{1,0:T(8,128)} fusion(bf16[616,8192]{1,0:T(8,128)(2,1)} %param.11, f32[616,8]{0,1:T(8,128)S(1)} %copy-done.3, f32[8,8192]{1,0:T(8,128)S(1)} %copy-done), kind=kOutput, calls=%fused_computation.7 | convolution fusion | flops 494534656 | bytes 30559488 | tf_op jit(solution)/shard_map/dot_general | solution.py:27
  73.6 33.1 %gather_fusion.1 = bf16[8192,384]{1,0:T(8,128)(2,1)} fusion(bf16[1024,384]{1,0:T(8,128)(2,1)S(1)} %bitcast.45, s32[8192]{0:T(1024)S(1)} %fusion.12), kind=kCustom, calls=%fused_computation.1 | custom fusion | bytes 12615680 | tf_op jit(solution)/shard_map/gather | solution.py:65
  106.6 24.5 %fusion.2 = f32[8,1024,384]{2,1,0:T(8,128)} fusion(bf16[8,616,384]{2,1,0:T(8,128)(2,1)} %param.10, f32[77,8,8,1024]{3,2,1,0:T(8,128)} %bitcast.47, f32[616,8]{0,1:T(8,128)S(1)} %multiply_bitcast_fusion, bf16[8,1024,384]{2,1,0:T(8,128)(2,1)} %bitcast.50), kind=kOutput, calls=%fused_computation.8 | convolution fusion | flops 7766212608 | bytes 42863872 | tf_op jit(solution)/shard_map/tcf,cto->tof/dot_general | solution.py:36
  131.2 50.4 %scatter_custom_fusion = f32[1024,384]{1,0:T(8,128)} fusion(s32[8192]{0:T(1024)S(1)} %copy-done.2, f32[8192,384]{1,0:T(8,128)} %bitcast.55, f32[]{:T(128)} %constant.4.clone.1), kind=kCustom, calls=%fused_computation.14 | custom fusion | flops 3145728 | bytes 1573376 | tf_op jit(solution)/shard_map/scatter-add | solution.py:67
  181.6 9.8 %all-to-all-start.2 = ((f32[128,8,384]{2,1,0:T(8,128)}), f32[128,8,384]{2,1,0:T(8,128)S(1)}, u32[]{:S(2)}, u32[]{:S(2)}) async-start(f32[128,8,384]{2,1,0:T(8,128)} %bitcast.12), calls=%async_computation.2 | async-start | bytes 3145728 | tf_op jit(solution)/shard_map/all_to_all | solution.py:12
  191.4 0.1 copy.30
  191.6 24.5 %all-to-all-done.2 = f32[128,8,384]{2,1,0:T(8,128)S(1)} async-done(((f32[128,8,384]{2,1,0:T(8,128)}), f32[128,8,384]{2,1,0:T(8,128)S(1)}, u32[]{:S(2)}, u32[]{:S(2)}) %all-to-all-start.2) | async-done | bytes 1572896 | tf_op jit(solution)/shard_map/all_to_all | solution.py:12
  216.1 7.1 %scatter_custom_fusion.1 = f32[1024,384]{1,0:T(8,128)S(1)} fusion(s32[1024]{0:T(1024)S(1)} %reshape.89, f32[128,8,384]{2,1,0:T(8,128)S(1)} %all-to-all-done.2, f32[]{:T(128)} %constant.4.clone.1), kind=kCustom, calls=%fused_computation.11 | custom fusion | flops 393216 | bytes 3145732 | tf_op jit(solution)/shard_map/scatter-add | solution.py:69
  223.2 0.5 copy.37
  223.6 1.1 copy.38
  224.7 27.4 %all_to_all.43 = f32[3,128,1024]{2,0,1:T(4,128)S(1)} all-to-all(f32[3,128,1024]{2,0,1:T(4,128)S(1)} %copy.38), channel_id=1, replica_groups=mesh['lev'=4,'col'=32] {'lev'}, dimensions={1} | all-to-all | bytes 3145728 | tf_op jit(solution)/shard_map/all_to_all | solution.py:75
  252.2 0.9 copy.39
  253.1 1.3 copy.44
  (21 shorter events, 0.2 us)
Async XLA Ops:
  0.0 52.8 %copy-start = (f32[8,8192]{1,0:T(8,128)S(1)}, f32[8,8192]{1,0:T(8,128)}, u32[]{:S(2)}) copy-start(f32[8,8192]{1,0:T(8,128)} %param.12) | copy-start | bytes 786436
  6.0 10.6 %copy-start.5 = (s32[1,128,8]{1,2,0:T(8,128)S(1)}, s32[1,128,8]{1,2,0:T(8,128)}, u32[]{:S(2)}) copy-start(s32[1,128,8]{1,2,0:T(8,128)} %param.16) | copy-start | bytes 12292
  6.0 10.8 %copy-start.6 = (f32[616]{0:T(1024)S(1)}, f32[616]{0:T(1024)}, u32[]{:S(2)}) copy-start(f32[616]{0:T(1024)} %param.14) | copy-start | bytes 7396
  6.0 10.8 %copy-start.4 = (s32[8,616]{1,0:T(8,128)S(1)}, s32[8,616]{1,0:T(8,128)}, u32[]{:S(2)}) copy-start(s32[8,616]{1,0:T(8,128)} %param.15) | copy-start | bytes 59140
  6.0 10.9 %copy-start.2 = (s32[8192]{0:T(1024)S(1)}, s32[8192]{0:T(1024)}, u32[]{:S(2)}) copy-start(s32[8192]{0:T(1024)} %param.17) | copy-start | bytes 98308
  11.6 16.4 %all-to-all-start = ((bf16[4,2,49152]{2,1,0:T(2,128)(2,1)}), bf16[4,2,49152]{2,1,0:T(2,128)(2,1)S(1)}, u32[]{:S(2)}, u32[]{:S(2)}) async-start(bf16[4,2,49152]{2,1,0:T(2,128)(2,1)} %reshape.103), calls=%async_computation | async-start | bytes 1572864 | tf_op jit(solution)/shard_map/all_to_all | solution.py:57
  37.9 14.9 %copy-start.3 = (f32[616,8]{0,1:T(8,128)S(1)}, f32[616,8]{0,1:T(8,128)}, u32[]{:S(2)}) copy-start(f32[616,8]{0,1:T(8,128)} %param.13) | copy-start | bytes 59140
  42.9 30.6 %all-to-all-start.1 = ((bf16[128,8,384]{2,1,0:T(8,128)(2,1)}), bf16[128,8,384]{2,1,0:T(8,128)(2,1)S(1)}, u32[]{:S(2)}, u32[]{:S(2)}) async-start(bf16[128,8,384]{2,1,0:T(8,128)(2,1)} %bitcast.7), calls=%async_computation.1 | async-start | bytes 1572864 | tf_op jit(solution)/shard_map/all_to_all | solution.py:8
  181.6 34.5 %all-to-all-start.2 = ((f32[128,8,384]{2,1,0:T(8,128)}), f32[128,8,384]{2,1,0:T(8,128)S(1)}, u32[]{:S(2)}, u32[]{:S(2)}) async-start(f32[128,8,384]{2,1,0:T(8,128)} %bitcast.12), calls=%async_computation.2 | async-start | bytes 3145728 | tf_op jit(solution)/shard_map/all_to_all | solution.py:12
  224.7 29.7 %copy-start.1 = (f32[8,8192]{1,0:T(8,128)S(1)}, f32[8,8192]{1,0:T(8,128)}, u32[]{:S(2)}) copy-start(f32[8,8192]{1,0:T(8,128)} %param.12) | copy-start | bytes 786436
where the time goes:
time: 256 us; the launch traced here: 254 us
  local copies, waits for them, and re-layouts  63.8 us (25%)
  other arithmetic  57.5 us (22%)
  matrix products  45.3 us (18%)
  waiting for transfers between devices  35.6 us (14%)
  blocking collectives  27.4 us (11%)
  starting transfers between devices  24.6 us (10%)
    scatter-add x1, other arithmetic, on_device(): jax.ops.segment_sum(adjoint, obs_slot, num_segments=peer_count * capacity)  50.4 us
    gather x1, local copies, waits for them, and re-layouts, on_device(): profile = incoming[obs_slot]  33.1 us
    all_to_all x1, blocking collectives, on_device(): lax.all_to_all(field_adjoint, 'lev', split_axis=1, concat_axis=2, tiled=T...  27.4 us
    dot_general x1, matrix products, observe(): jnp.einsum('tcf,cto->tof', jacobian, forcing, preferred_element_type=jnp....  24.5 us
    all_to_all x1, waiting for transfers between devices, return_rows(): lax.all_to_all(outgoing, ('lev', 'col'), split_axis=0, concat_axis=0, til...  24.5 us
    dot_general x1, matrix products, observe(): jnp.dot(bias_coef, predictor, precision=lax.Precision.HIGHEST, preferred_...  20.8 us
    unnamed x18, local copies, waits for them, and re-layouts  15.9 us
    all_to_all x1, waiting for transfers between devices, on_device(): lax.all_to_all(increment, 'lev', split_axis=2, concat_axis=1, tiled=True)  11.1 us
  transfers between devices with their start and end apart: 3, of which 2 were waited for; matrix products, arithmetic and copies ran while one was open for 8% of the time, Pallas kernels for 0%

commit v1 on v0

v1 whole, which is shorter than its diff:
```python
import functools

import jax
import jax.numpy as jnp
from jax import lax
from jax.experimental import pallas as pl
from jax.experimental.pallas import tpu as pltpu
from jax.sharding import PartitionSpec as P

MESH = pl.DeviceIdType.MESH
NF = 3
LEVD = 4
COLD = 32
NDEV = LEVD * COLD
SLAB = 32
ROWS = NF * SLAB
PROF = ROWS * LEVD
CAP = 8
SLOTS = NDEV * CAP
COLS = 1024
CHAN = 616
CPAD = 640
NPRED = 8
TILE = 1024
TILES = 8
OBS = TILE * TILES
F32 = jnp.float32
BF16 = jnp.bfloat16


def peer_id(index):
    return (index // COLD, lax.rem(index, COLD))


def one_hot(row, block):
    local = jnp.broadcast_to((row - 256.0 * block), (256, 128)).astype(BF16)
    index = lax.broadcasted_iota(jnp.int32, (256, 128), 0).astype(F32).astype(BF16)
    return jnp.where(index == local, jnp.ones((), BF16), jnp.zeros((), BF16))


def split3(value):
    high = value.astype(BF16).astype(F32)
    rest = value - high
    mid = rest.astype(BF16).astype(F32)
    return high, mid, (rest - mid).astype(BF16).astype(F32)


def kernel(
    inc_hbm, jac_hbm, dep_hbm, pred_hbm, coef_hbm, sigma_hbm, use_hbm, cols_hbm, slot_hbm,
    out_ref,
    inc, dep, pred, coef, sigma, use, cols, slot,
    lists, hot, gath, sendb, recvb, xt, xaug, jaug, jt, paug, scale, square, forcing,
    adj, acc, rsend, rrecv, yt,
    in_sem, dep_sem, list_send, list_recv, send_sem, recv_sem, rsend_sem, rrecv_sem, own_sem,
):
    lev = lax.axis_index("lev")
    col = lax.axis_index("col")
    me = lev * COLD + col
    barrier = pltpu.get_barrier_semaphore()

    loads = [
        pltpu.make_async_copy(src, dst, in_sem.at[i])
        for i, (src, dst) in enumerate(
            (
                (cols_hbm, cols), (inc_hbm, inc), (slot_hbm, slot), (jac_hbm, jaug.at[:, :, pl.ds(0, PROF)]), (pred_hbm, pred),
                (coef_hbm, coef), (sigma_hbm, sigma), (use_hbm, use),
            )
        )
    ]
    for load in loads:
        load.start()

    def dep_load(t):
        at = pl.multiple_of(t * TILE, TILE)
        return pltpu.make_async_copy(
            dep_hbm.at[:, pl.ds(at, TILE)], dep.at[lax.rem(t, 2)], dep_sem.at[lax.rem(t, 2)]
        )

    dep_load(0).start()

    def greet(i, carry):
        pl.semaphore_signal(barrier, inc=1, device_id=peer_id(lax.rem(me + i, NDEV)), device_id_type=MESH)
        return carry

    lax.fori_loop(1, NDEV, greet, 0)

    loads[0].wait()
    square[...] = jnp.zeros_like(square)
    square[0:NDEV, 0:CAP] = cols[...].astype(F32)
    lists[lev] = square[0:128, :].T[0:CAP, :].astype(jnp.int32)
    pl.semaphore_wait(barrier, NDEV - 1)

    def list_copy(i):
        other = lax.rem(lev + i, LEVD)
        return pltpu.make_async_remote_copy(
            src_ref=lists.at[lev], dst_ref=lists.at[lev], send_sem=list_send.at[i],
            recv_sem=list_recv.at[i], device_id=(other, col), device_id_type=MESH,
        )

    for i in range(1, LEVD):
        list_copy(i).start()
    loads[1].wait()

    def build_pick(owner):
        def build(k, carry):
            row = lists[owner, pl.ds(k, 1), :].astype(F32)
            at = pl.multiple_of(owner * SLOTS + k * 128, 128)
            for b in range(4):
                hot[b * 256 : (b + 1) * 256, pl.ds(at, 128)] = one_hot(row, b)
            return carry

        lax.fori_loop(0, CAP, build, 0)

    for i in range(LEVD):
        owner = lax.rem(lev + (LEVD - i), LEVD)
        if i:
            list_copy(i).wait_recv()

        build_pick(owner)
        at = pl.multiple_of(owner * COLS, COLS)
        to = pl.multiple_of(owner * ROWS, 32)
        gath[pl.ds(to, ROWS), :] = jnp.dot(
            inc[:, pl.ds(at, COLS)], hot[:, pl.ds(at, SLOTS)], preferred_element_type=F32
        )
    for i in range(1, LEVD):
        list_copy(i).wait_send()
    for k in range(CAP):
        for m in range(NF):
            rsend[m, pl.ds(k, NDEV, stride=CAP), :] = gath[m * 128 : (m + 1) * 128, k * 128 : (k + 1) * 128].T
    for m in range(NF):
        sendb[:, :, m * 128 : (m + 1) * 128] = rsend[m].reshape(NDEV, CAP, 128).astype(BF16)

    own = pltpu.make_async_copy(sendb.at[me], recvb.at[me], own_sem.at[0])
    own.start()

    def fetch(i, carry):
        other = lax.rem(me + i, NDEV)
        pltpu.make_async_remote_copy(
            src_ref=sendb.at[other], dst_ref=recvb.at[me], send_sem=send_sem, recv_sem=recv_sem,
            device_id=peer_id(other), device_id_type=MESH,
        ).start()
        return carry

    lax.fori_loop(1, NDEV, fetch, 0)

    for load in loads[2:]:
        load.wait()

    def build_hot(m, carry):
        row = slot[pl.ds(m, 1), :].astype(F32)
        at = pl.multiple_of(m * 128, 128)
        for b in range(4):
            hot[b * 256 : (b + 1) * 256, pl.ds(at, 128)] = one_hot(row, b)
        return carry

    lax.fori_loop(0, OBS // 128, build_hot, 0)

    inverse = 1.0 / (sigma[...] * sigma[...])
    square[...] = jnp.zeros_like(square)
    wide = jnp.concatenate(
        [use[...].astype(F32) * inverse, jnp.zeros((TILES, CPAD - CHAN), F32)], axis=1
    )
    for m in range(CPAD // 128):
        square[0:TILES, :] = wide[:, m * 128 : (m + 1) * 128]
        turned = square[0:128, :].T
        for t in range(TILES):
            scale[t, m * 128 : (m + 1) * 128, :] = jnp.broadcast_to(turned[:, t : t + 1], (128, 128))

    high, mid, low = split3(pred[...])
    paug[...] = jnp.zeros_like(paug)
    paug[0:48, :] = jnp.concatenate([high, mid, low, high, mid, high], axis=0).astype(BF16)
    repeat = (
        lax.broadcasted_iota(jnp.int32, (NPRED, 128), 0)
        == lax.rem(lax.broadcasted_iota(jnp.int32, (NPRED, 128), 1), NPRED)
    ).astype(F32)
    tiled = jnp.dot(coef[...], repeat, precision=lax.Precision.HIGHEST, preferred_element_type=F32)
    ch, cm, cl = split3(tiled)
    lane = lax.broadcasted_iota(jnp.int32, (CHAN, 128), 1)
    ccoef = jnp.where(lane < 24, ch, jnp.where(lane < 40, cm, jnp.where(lane < 48, cl, 0.0)))

    forcing[...] = jnp.zeros_like(forcing)
    for t in range(TILES):
        jaug[t, :, PROF : PROF + 128] = ccoef.astype(BF16)

    def turn(t, carry):
        tall = jnp.concatenate([jaug[t, :, 0:PROF].astype(F32), jnp.zeros((CPAD - CHAN, PROF), F32)], axis=0)
        jt[t] = tall.T.astype(BF16)
        return carry

    lax.fori_loop(0, TILES, turn, 0)

    pltpu.make_async_copy(sendb.at[pl.ds(0, NDEV - 1)], sendb.at[pl.ds(0, NDEV - 1)], send_sem).wait()
    pltpu.make_async_copy(recvb.at[pl.ds(0, NDEV - 1)], recvb.at[pl.ds(0, NDEV - 1)], recv_sem).wait()
    own.wait()
    for h in range(LEVD):
        got = recvb[h * COLD : (h + 1) * COLD].astype(F32).reshape(COLD * CAP, PROF)
        turned = got.T.astype(BF16)
        for owner in range(LEVD):
            for field in range(NF):
                xt[field * 128 + h * SLAB : field * 128 + (h + 1) * SLAB, owner * 256 : (owner + 1) * 256] = turned[
                    owner * ROWS + field * SLAB : owner * ROWS + (field + 1) * SLAB, :
                ]

    def observe(t, carry):
        @pl.when(t + 1 < TILES)
        def _():
            dep_load(t + 1).start()

        at = pl.multiple_of(t * TILE, TILE)
        xaug[0:PROF, :] = jnp.dot(xt[...], hot[:, pl.ds(at, TILE)], preferred_element_type=F32).astype(BF16)
        xaug[PROF : PROF + 128, :] = paug[:, pl.ds(at, TILE)]
        dep_load(t).wait()
        half = lax.rem(t, 2)
        for n in range(TILE // 256):
            lanes = slice(n * 256, (n + 1) * 256)
            tangent = jnp.dot(jaug[t], xaug[:, lanes], preferred_element_type=F32)
            factor = scale[t, 0:CHAN, :]
            residual = tangent - dep[half, :, lanes].astype(F32)
            forcing[0:CHAN, lanes] = (jnp.concatenate([factor, factor], axis=1) * residual).astype(BF16)
        for n in range(TILE // 256):
            lanes = slice(n * 256, (n + 1) * 256)
            to = pl.multiple_of(at + n * 256, 256)
            value = jnp.dot(jt[t], forcing[:, lanes], preferred_element_type=F32)
            first = value.astype(BF16)
            second = (value - first.astype(F32)).astype(BF16)
            for h in range(LEVD):
                for field in range(NF):
                    rows = slice(field * 128 + h * SLAB, field * 128 + (h + 1) * SLAB)
                    put = slice(field * SLAB, (field + 1) * SLAB)
                    adj[h, 0, put, pl.ds(to, 256)] = first[rows, :]
                    adj[h, 1, put, pl.ds(to, 256)] = second[rows, :]
        return carry

    lax.fori_loop(0, TILES, observe, 0)

    def give_back(step, carry):
        pair = lax.rem(lev // 2 + step // 2, 2)
        half = lax.rem(col // 16 + step, 2)
        acc[...] = jnp.zeros_like(acc)

        def add(t, inner):
            at = pl.multiple_of(t * TILE, TILE)
            left = adj[pl.ds(pair * 2, 2), :, :, pl.ds(at, TILE)].reshape(4 * ROWS, TILE)
            for owner in range(LEVD):
                rows = pl.multiple_of(owner * 256 + half * 128, 128)
                acc[:, owner * 128 : (owner + 1) * 128] += lax.dot_general(
                    left, hot[pl.ds(rows, 128), pl.ds(at, TILE)], (((1,), (1,)), ((), ())),
                    preferred_element_type=F32,
                )
            return inner

        lax.fori_loop(0, TILES, add, 0)
        for h in range(2):
            total = acc[h * 192 : h * 192 + ROWS, :] + acc[h * 192 + ROWS : (h + 1) * 192, :]
            tall = jnp.concatenate([total[:, o * 128 : (o + 1) * 128] for o in range(LEVD)], axis=0)
            to = pl.multiple_of(((pair * 2 + h) * COLD + half * 16) * CAP, 128)
            for m in range(NF):
                rsend[m, pl.ds(to, 128), :] = tall[m * 128 : (m + 1) * 128, :].T

        def push(i, inner):
            other = (pair * 2 + i // 16) * COLD + half * 16 + lax.rem(i + col, 16)
            src = rsend.at[:, pl.ds(pl.multiple_of(other * CAP, CAP), CAP), :]
            dst = rrecv.at[:, pl.ds(pl.multiple_of(me * CAP, CAP), CAP), :]

            @pl.when(other != me)
            def _():
                pltpu.make_async_remote_copy(
                    src_ref=src, dst_ref=dst, send_sem=rsend_sem, recv_sem=rrecv_sem,
                    device_id=peer_id(other), device_id_type=MESH,
                ).start()

            @pl.when(other == me)
            def _():
                pltpu.make_async_copy(src, dst, own_sem.at[1]).start()

            return inner

        lax.fori_loop(0, 32, push, 0)
        return carry

    lax.fori_loop(0, 4, give_back, 0)
    for owner in range(LEVD):
        build_pick(owner)
    mine = pl.ds(pl.multiple_of(me * CAP, CAP), CAP)
    pltpu.make_async_copy(rsend.at[:, mine, :], rrecv.at[:, mine, :], own_sem.at[1]).wait()
    most = pl.ds(0, SLOTS - CAP)
    pltpu.make_async_copy(rsend.at[:, most, :], rsend.at[:, most, :], rsend_sem).wait()
    pltpu.make_async_copy(rrecv.at[:, most, :], rrecv.at[:, most, :], rrecv_sem).wait()

    for k in range(CAP):
        value = jnp.concatenate([rrecv[m, pl.ds(k, NDEV, stride=CAP), :].T for m in range(NF)], axis=0)
        first = value.astype(BF16)
        second = (value - first.astype(F32)).astype(BF16)
        lanes = slice(k * 128, (k + 1) * 128)
        for owner in range(LEVD):
            rows = slice(owner * ROWS, (owner + 1) * ROWS)
            yt[owner, 0:ROWS, lanes] = first[rows, :]
            yt[owner, ROWS : 2 * ROWS, lanes] = second[rows, :]
    for owner in range(LEVD):
        both = lax.dot_general(
            yt[owner], hot[:, owner * SLOTS : (owner + 1) * SLOTS], (((1,), (1,)), ((), ())), preferred_element_type=F32
        )
        out_ref[:, owner * COLS : (owner + 1) * COLS] = both[0:ROWS, :] + both[ROWS : 2 * ROWS, :]


def on_device(increment, jacobian, departure, predictor, bias_coef, obs_sigma, channel_use, send_cols, obs_slot):
    out = pl.pallas_call(
        kernel,
        out_shape=jax.ShapeDtypeStruct((ROWS, LEVD * COLS), F32),
        in_specs=[pl.BlockSpec(memory_space=pl.ANY)] * 9,
        out_specs=pl.BlockSpec(memory_space=pltpu.VMEM),
        scratch_shapes=[
            pltpu.VMEM((ROWS, LEVD * COLS), BF16),
            pltpu.VMEM((2, CHAN, TILE), BF16),
            pltpu.VMEM((NPRED, OBS), F32),
            pltpu.VMEM((CHAN, NPRED), F32),
            pltpu.VMEM((1, CHAN), F32),
            pltpu.VMEM((TILES, CHAN), jnp.int32),
            pltpu.VMEM((NDEV, CAP), jnp.int32),
            pltpu.VMEM((OBS // 128, 128), jnp.int32),
            pltpu.VMEM((LEVD, CAP, NDEV), jnp.int32),
            pltpu.VMEM((SLOTS, OBS), BF16),
            pltpu.VMEM((PROF, SLOTS), F32),
            pltpu.VMEM((NDEV, CAP, PROF), BF16),
            pltpu.VMEM((NDEV, CAP, PROF), BF16),
            pltpu.VMEM((PROF, SLOTS), BF16),
            pltpu.VMEM((PROF + 128, TILE), BF16),
            pltpu.VMEM((TILES, CHAN, PROF + 128), BF16),
            pltpu.VMEM((TILES, PROF, CPAD), BF16),
            pltpu.VMEM((128, OBS), BF16),
            pltpu.VMEM((TILES, CPAD, 128), F32),
            pltpu.VMEM((128, 128), F32),
            pltpu.VMEM((CPAD, TILE), BF16),
            pltpu.VMEM((LEVD, 2, ROWS, OBS), BF16),
            pltpu.VMEM((4 * ROWS, 512), F32),
            pltpu.VMEM((NF, SLOTS, 128), F32),
            pltpu.VMEM((NF, SLOTS, 128), F32),
            pltpu.VMEM((LEVD, 2 * ROWS, SLOTS), BF16),
            pltpu.SemaphoreType.DMA((8,)),
            pltpu.SemaphoreType.DMA((2,)),
            pltpu.SemaphoreType.DMA((LEVD,)),
            pltpu.SemaphoreType.DMA((LEVD,)),
            pltpu.SemaphoreType.DMA,
            pltpu.SemaphoreType.DMA,
            pltpu.SemaphoreType.DMA,
            pltpu.SemaphoreType.DMA,
            pltpu.SemaphoreType.DMA((2,)),
        ],
        compiler_params=pltpu.CompilerParams(
            collective_id=0, has_side_effects=True, vmem_limit_bytes=63 * 2**20
        ),
    )(
        increment.reshape(ROWS, LEVD * COLS),
        jacobian,
        departure,
        predictor,
        bias_coef,
        obs_sigma.reshape(1, CHAN),
        channel_use,
        send_cols.reshape(NDEV, CAP),
        obs_slot.reshape(OBS // 128, 128),
    )
    return out.reshape(NF, SLAB, LEVD * COLS)


def solution(mesh):
    return jax.shard_map(
        on_device,
        mesh=mesh,
        in_specs=(
            P(None, "lev", "col"),
            P(("lev", "col"), None, None),
            P(None, ("lev", "col")),
            P(None, ("lev", "col")),
            P(),
            P(),
            P(("lev", "col"), None),
            P(("lev", "col"), None, None),
            P(("lev", "col")),
        ),
        out_specs=P(None, "lev", "col"),
        check_vma=False,
    )
```

time: 256 us -> 110 us (0.43)
  Pallas kernels: 0 us -> 102 us
  other arithmetic: 57.5 us -> 0 us
  local copies, waits for them, and re-layouts: 63.8 us -> 6.93 us
  matrix products: 45.3 us -> 0 us
  waiting for transfers between devices: 35.6 us -> 0 us
  blocking collectives: 27.4 us -> 0 us
  starting transfers between devices: 24.6 us -> 0 us
    pallas_call x0 -> x1, Pallas kernels: none -> 102 us  [on_device(): pl.pallas_call(kernel, out_shape=jax.ShapeDtypeStruct((ROWS, LEVD * COLS)...]
    scatter-add x2 -> x0, other arithmetic: 57.5 us -> none  [the longest x1 50.4 us: on_device(): jax.ops.segment_sum(adjoint, obs_slot, num_segments=peer_count * capacity)]
    dot_general x2 -> x0, matrix products: 45.3 us -> none  [the longest x1 24.5 us: observe(): jnp.einsum('tcf,cto->tof', jacobian, forcing, preferred_element_type=jnp....]
    gather x2 -> x0, local copies, waits for them, and re-layouts: 38.1 us -> none  [the longest x1 33.1 us: on_device(): profile = incoming[obs_slot]]
    all_to_all x3 -> x0, waiting for transfers between devices: 35.6 us -> none  [the longest x1 24.5 us: return_rows(): lax.all_to_all(outgoing, ('lev', 'col'), split_axis=0, concat_axis=0, til...]
    all_to_all x1 -> x0, blocking collectives: 27.4 us -> none  [on_device(): lax.all_to_all(field_adjoint, 'lev', split_axis=1, concat_axis=2, tiled=T...]
    all_to_all x3 -> x0, starting transfers between devices: 24.6 us -> none  [the longest x1 9.84 us: fetch_rows(): lax.all_to_all(outgoing, ('lev', 'col'), split_axis=0, concat_axis=0, til...]
    unnamed x18 -> x3, local copies, waits for them, and re-layouts: 15.9 us -> 5.66 us
  transfers between devices with their start and end apart: 3 -> 0, of which waited for: 2 -> 0; matrix products, arithmetic and copies ran while one was open for 8% -> 0% of each run, Pallas kernels for 0% -> 0%
where the time goes in v1:
time: 110 us; the launch traced here: 109 us
  Pallas kernels  102 us (93%)
  local copies, waits for them, and re-layouts  6.93 us (6%)
    pallas_call x1, Pallas kernels, on_device(): pl.pallas_call(kernel, out_shape=jax.ShapeDtypeStruct((ROWS, LEVD * COLS)...  102 us
    unnamed x3, local copies, waits for them, and re-layouts  5.66 us

profile of v1, /device:TPU:1, one launch (start us, length us, event | category | flops | bytes accessed | tf_op | source)
XLA Modules:
  0.0 109.4 jit_solution(10056242340576199389)
XLA Ops:
  0.0 1.3 %reshape.16.sigma_hbm = f32[1,616]{1,0:T(1,128)} reshape(f32[616]{0:T(1024)} %param.14) | data formatting | bytes 4928 | tf_op jit(solution)/shard_map/reshape | solution.py:358
  1.3 1.4 %copy.10 = s32[1,128,8]{2,1,0:T(8,128)} copy(s32[1,128,8]{1,2,0:T(8,128)} %param.16) | data formatting | bytes 8192 | tf_op args[7]
  2.7 1.6 %copy.11.coef_hbm = f32[616,8]{1,0:T(8,128)} copy(f32[616,8]{0,1:T(8,128)} %param.13) | data formatting | bytes 39424 | tf_op args[4]
  4.3 102.5 %shard_map.91 = f32[96,4096]{1,0:T(8,128)} custom-call(bf16[96,4096]{1,0:T(8,128)(2,1)} %bitcast.5, bf16[8,616,384]{2,1,0:T(8,128)(2,1)} %jac_hbm.1, bf16[616,8192]{1,0:T(8,128)(2,1)} %dep_hbm.1, f32[8,8192]{1,0:T(8,128)} %pred_hbm.1, f32[616,8]{1,0:T(8,128)} %copy.11.coef_hbm, f32[1,616]{1,0:T(1,128)} %reshape.16.sigma_hbm, s32[8,616]{1,0:T(8,128)} %use_hbm.1, ...), custom_call_target="tpu_custom_call" | custom-call | tf_op jit(solution)/shard_map/pallas_call | solution.py:307
  106.8 2.7 %copy.13 = f32[3,32,4096]{2,1,0:T(8,128)} copy(f32[3,32,4096]{2,1,0:T(8,128)} %bitcast.4) | data formatting | bytes 3145728

commit v2 on v1

--- a/solution.py
+++ b/solution.py
@@ -48,10 +48,10 @@
 def kernel(
     inc_hbm, jac_hbm, dep_hbm, pred_hbm, coef_hbm, sigma_hbm, use_hbm, cols_hbm, slot_hbm,
     out_ref,
-    inc, dep, pred, coef, sigma, use, cols, slot,
+    inc, dep, pred, coef, sigma, use, slot,
     lists, hot, gath, sendb, recvb, xt, xaug, jaug, jt, paug, scale, square, forcing,
-    adj, acc, rsend, rrecv, yt,
-    in_sem, dep_sem, list_send, list_recv, send_sem, recv_sem, rsend_sem, rrecv_sem, own_sem,
+    adj, acc, rsend, rrecv, units_out, units_in, rows8, yt,
+    in_sem, dep_sem, list_send, list_recv, send_sem, recv_sem, rsend_sem, rrecv_sem, msend_sem, mrecv_sem, all_sem, own_sem,
 ):
     lev = lax.axis_index("lev")
     col = lax.axis_index("col")
@@ -62,7 +62,7 @@
         pltpu.make_async_copy(src, dst, in_sem.at[i])
         for i, (src, dst) in enumerate(
             (
-                (cols_hbm, cols), (inc_hbm, inc), (slot_hbm, slot), (jac_hbm, jaug.at[:, :, pl.ds(0, PROF)]), (pred_hbm, pred),
+                (cols_hbm, lists.at[lev]), (inc_hbm, inc), (slot_hbm, slot), (jac_hbm, jaug.at[:, :, pl.ds(0, PROF)]), (pred_hbm, pred),
                 (coef_hbm, coef), (sigma_hbm, sigma), (use_hbm, use),
             )
         )
@@ -78,17 +78,21 @@
 
     dep_load(0).start()
 
-    def greet(i, carry):
-        pl.semaphore_signal(barrier, inc=1, device_id=peer_id(lax.rem(me + i, NDEV)), device_id_type=MESH)
-        return carry
-
-    lax.fori_loop(1, NDEV, greet, 0)
-
+    place = col // 2
+    core = lax.rem(col, 2)
+
+    def near(i):
+        return (lax.rem(lev + i // 2, LEVD), place * 2 + lax.rem(core + i, 2))
+
+    def far(i):
+        return (lev, lax.rem(place + i, COLD // 2) * 2 + core)
+
+    for i in range(1, 2 * LEVD):
+        pl.semaphore_signal(barrier, inc=1, device_id=near(i), device_id_type=MESH)
+    for i in range(1, COLD // 2):
+        pl.semaphore_signal(barrier, inc=1, device_id=far(i), device_id_type=MESH)
     loads[0].wait()
-    square[...] = jnp.zeros_like(square)
-    square[0:NDEV, 0:CAP] = cols[...].astype(F32)
-    lists[lev] = square[0:128, :].T[0:CAP, :].astype(jnp.int32)
-    pl.semaphore_wait(barrier, NDEV - 1)
+    pl.semaphore_wait(barrier, 2 * LEVD - 1 + COLD // 2 - 1)
 
     def list_copy(i):
         other = lax.rem(lev + i, LEVD)
@@ -99,6 +103,8 @@
 
     for i in range(1, LEVD):
         list_copy(i).start()
+    for i in range(1, 2 * LEVD):
+        pl.semaphore_signal(all_sem, inc=1, device_id=near(i), device_id_type=MESH)
     loads[1].wait()
 
     def build_pick(owner):
@@ -126,10 +132,11 @@
         list_copy(i).wait_send()
     for k in range(CAP):
         for m in range(NF):
-            rsend[m, pl.ds(k, NDEV, stride=CAP), :] = gath[m * 128 : (m + 1) * 128, k * 128 : (k + 1) * 128].T
+            rows8[m, pl.ds(k, NDEV, stride=CAP), :] = gath[m * 128 : (m + 1) * 128, k * 128 : (k + 1) * 128].T
     for m in range(NF):
-        sendb[:, :, m * 128 : (m + 1) * 128] = rsend[m].reshape(NDEV, CAP, 128).astype(BF16)
-
+        sendb[:, :, m * 128 : (m + 1) * 128] = rows8[m].reshape(NDEV, CAP, 128).astype(BF16)
+
+    pl.semaphore_wait(all_sem, 2 * LEVD - 1)
     own = pltpu.make_async_copy(sendb.at[me], recvb.at[me], own_sem.at[0])
     own.start()
 
@@ -155,7 +162,8 @@
 
     lax.fori_loop(0, OBS // 128, build_hot, 0)
 
-    inverse = 1.0 / (sigma[...] * sigma[...])
+    deviation = sigma[...].reshape(1, CHAN)
+    inverse = 1.0 / (deviation * deviation)
     square[...] = jnp.zeros_like(square)
     wide = jnp.concatenate(
         [use[...].astype(F32) * inverse, jnp.zeros((TILES, CPAD - CHAN), F32)], axis=1
@@ -173,7 +181,9 @@
         lax.broadcasted_iota(jnp.int32, (NPRED, 128), 0)
         == lax.rem(lax.broadcasted_iota(jnp.int32, (NPRED, 128), 1), NPRED)
     ).astype(F32)
-    tiled = jnp.dot(coef[...], repeat, precision=lax.Precision.HIGHEST, preferred_element_type=F32)
+    tiled = lax.dot_general(
+        coef[...], repeat, (((0,), (0,)), ((), ())), precision=lax.Precision.HIGHEST, preferred_element_type=F32
+    )
     ch, cm, cl = split3(tiled)
     lane = lax.broadcasted_iota(jnp.int32, (CHAN, 128), 1)
     ccoef = jnp.where(lane < 24, ch, jnp.where(lane < 40, cm, jnp.where(lane < 48, cl, 0.0)))
@@ -241,37 +251,47 @@
         def add(t, inner):
             at = pl.multiple_of(t * TILE, TILE)
             left = adj[pl.ds(pair * 2, 2), :, :, pl.ds(at, TILE)].reshape(4 * ROWS, TILE)
-            for owner in range(LEVD):
-                rows = pl.multiple_of(owner * 256 + half * 128, 128)
-                acc[:, owner * 128 : (owner + 1) * 128] += lax.dot_general(
-                    left, hot[pl.ds(rows, 128), pl.ds(at, TILE)], (((1,), (1,)), ((), ())),
-                    preferred_element_type=F32,
-                )
+            right = jnp.concatenate(
+                [
+                    hot[pl.ds(pl.multiple_of(owner * 256 + half * 128, 128), 128), pl.ds(at, TILE)]
+                    for owner in range(LEVD)
+                ],
+                axis=0,
+            )
+            acc[...] += lax.dot_general(
+                left, right, (((1,), (1,)), ((), ())), preferred_element_type=F32
+            )
             return inner
 
         lax.fori_loop(0, TILES, add, 0)
         for h in range(2):
             total = acc[h * 192 : h * 192 + ROWS, :] + acc[h * 192 + ROWS : (h + 1) * 192, :]
             tall = jnp.concatenate([total[:, o * 128 : (o + 1) * 128] for o in range(LEVD)], axis=0)
-            to = pl.multiple_of(((pair * 2 + h) * COLD + half * 16) * CAP, 128)
-            for m in range(NF):
-                rsend[m, pl.ds(to, 128), :] = tall[m * 128 : (m + 1) * 128, :].T
+            unit = jnp.max(jnp.abs(tall), axis=0, keepdims=True) * (1.0 / 32767.0)
+            per = jnp.where(unit > 1e-37, 1.0 / unit, 0.0)
+            units_out[pair * 2 + h, half] = unit
+            code = jnp.round(tall * per).T.astype(jnp.int32).astype(jnp.int16)
+            rsend[pl.ds((pair * 2 + h) * COLD + half * 16, 16)] = code.reshape(16, CAP, PROF)
 
         def push(i, inner):
             other = (pair * 2 + i // 16) * COLD + half * 16 + lax.rem(i + col, 16)
-            src = rsend.at[:, pl.ds(pl.multiple_of(other * CAP, CAP), CAP), :]
-            dst = rrecv.at[:, pl.ds(pl.multiple_of(me * CAP, CAP), CAP), :]
+            moves = (
+                (rsend.at[other], rrecv.at[me], rsend_sem, rrecv_sem),
+                (units_out.at[pair * 2 + i // 16, half], units_in.at[me], msend_sem, mrecv_sem),
+            )
 
             @pl.when(other != me)
             def _():
-                pltpu.make_async_remote_copy(
-                    src_ref=src, dst_ref=dst, send_sem=rsend_sem, recv_sem=rrecv_sem,
-                    device_id=peer_id(other), device_id_type=MESH,
-                ).start()
+                for src, dst, send, receive in moves:
+                    pltpu.make_async_remote_copy(
+                        src_ref=src, dst_ref=dst, send_sem=send, recv_sem=receive,
+                        device_id=peer_id(other), device_id_type=MESH,
+                    ).start()
 
             @pl.when(other == me)
             def _():
-                pltpu.make_async_copy(src, dst, own_sem.at[1]).start()
+                for n, (src, dst, send, receive) in enumerate(moves):
+                    pltpu.make_async_copy(src, dst, own_sem.at[1 + n]).start()
 
             return inner
 
@@ -281,14 +301,21 @@
     lax.fori_loop(0, 4, give_back, 0)
     for owner in range(LEVD):
         build_pick(owner)
-    mine = pl.ds(pl.multiple_of(me * CAP, CAP), CAP)
-    pltpu.make_async_copy(rsend.at[:, mine, :], rrecv.at[:, mine, :], own_sem.at[1]).wait()
-    most = pl.ds(0, SLOTS - CAP)
-    pltpu.make_async_copy(rsend.at[:, most, :], rsend.at[:, most, :], rsend_sem).wait()
-    pltpu.make_async_copy(rrecv.at[:, most, :], rrecv.at[:, most, :], rrecv_sem).wait()
+    pltpu.make_async_copy(rsend.at[me], rrecv.at[me], own_sem.at[1]).wait()
+    pltpu.make_async_copy(units_in.at[me], units_in.at[me], own_sem.at[2]).wait()
+    most = pl.ds(0, NDEV - 1)
+    for sem in (msend_sem, mrecv_sem):
+        pltpu.make_async_copy(units_in.at[most], units_in.at[most], sem).wait()
+    pltpu.make_async_copy(rsend.at[most], rsend.at[most], rsend_sem).wait()
+    pltpu.make_async_copy(rrecv.at[most], rrecv.at[most], rrecv_sem).wait()
+    square[...] = units_in[:, 0, :].T
+    units = square[pl.ds(pl.multiple_of(lax.rem(col, 16) * CAP, CAP), CAP), :]
+    for m in range(NF):
+        rows8[m] = rrecv[:, :, m * 128 : (m + 1) * 128].astype(jnp.int32).astype(F32).reshape(SLOTS, 128)
 
     for k in range(CAP):
-        value = jnp.concatenate([rrecv[m, pl.ds(k, NDEV, stride=CAP), :].T for m in range(NF)], axis=0)
+        value = jnp.concatenate([rows8[m, pl.ds(k, NDEV, stride=CAP), :].T for m in range(NF)], axis=0)
+        value = value * units[k : k + 1, :]
         first = value.astype(BF16)
         second = (value - first.astype(F32)).astype(BF16)
         lanes = slice(k * 128, (k + 1) * 128)
@@ -313,10 +340,9 @@
             pltpu.VMEM((ROWS, LEVD * COLS), BF16),
             pltpu.VMEM((2, CHAN, TILE), BF16),
             pltpu.VMEM((NPRED, OBS), F32),
-            pltpu.VMEM((CHAN, NPRED), F32),
-            pltpu.VMEM((1, CHAN), F32),
+            pltpu.VMEM((NPRED, CHAN), F32),
+            pltpu.VMEM((CHAN,), F32),
             pltpu.VMEM((TILES, CHAN), jnp.int32),
-            pltpu.VMEM((NDEV, CAP), jnp.int32),
             pltpu.VMEM((OBS // 128, 128), jnp.int32),
             pltpu.VMEM((LEVD, CAP, NDEV), jnp.int32),
             pltpu.VMEM((SLOTS, OBS), BF16),
@@ -333,7 +359,10 @@
             pltpu.VMEM((CPAD, TILE), BF16),
             pltpu.VMEM((LEVD, 2, ROWS, OBS), BF16),
             pltpu.VMEM((4 * ROWS, 512), F32),
-            pltpu.VMEM((NF, SLOTS, 128), F32),
+            pltpu.VMEM((NDEV, CAP, PROF), jnp.int16),
+            pltpu.VMEM((NDEV, CAP, PROF), jnp.int16),
+            pltpu.VMEM((LEVD, 2, 1, 128), F32),
+            pltpu.VMEM((NDEV, 1, 128), F32),
             pltpu.VMEM((NF, SLOTS, 128), F32),
             pltpu.VMEM((LEVD, 2 * ROWS, SLOTS), BF16),
             pltpu.SemaphoreType.DMA((8,)),
@@ -344,7 +373,10 @@
             pltpu.SemaphoreType.DMA,
             pltpu.SemaphoreType.DMA,
             pltpu.SemaphoreType.DMA,
-            pltpu.SemaphoreType.DMA((2,)),
+            pltpu.SemaphoreType.DMA,
+            pltpu.SemaphoreType.DMA,
+            pltpu.SemaphoreType.REGULAR,
+            pltpu.SemaphoreType.DMA((3,)),
         ],
         compiler_params=pltpu.CompilerParams(
             collective_id=0, has_side_effects=True, vmem_limit_bytes=63 * 2**20
@@ -354,10 +386,10 @@
         jacobian,
         departure,
         predictor,
-        bias_coef,
-        obs_sigma.reshape(1, CHAN),
+        bias_coef.T,
+        obs_sigma,
         channel_use,
-        send_cols.reshape(NDEV, CAP),
+        send_cols.reshape(NDEV, CAP).T,
         obs_slot.reshape(OBS // 128, 128),
     )
     return out.reshape(NF, SLAB, LEVD * COLS)

time: 110 us -> 89.5 us (0.81)
  Pallas kernels: 102 us -> 86.7 us
  local copies, waits for them, and re-layouts: 6.93 us -> 2.65 us
    pallas_call x1, Pallas kernels: 102 us -> 86.7 us  [on_device(): pl.pallas_call(kernel, out_shape=jax.ShapeDtypeStruct((ROWS, LEVD * COLS)...]
    unnamed x3 -> x1, local copies, waits for them, and re-layouts: 5.66 us -> 2.65 us
    reshape x1 -> x0, local copies, waits for them, and re-layouts: 1.27 us -> none  [on_device(): obs_sigma.reshape(1, CHAN)]
where the time goes in v2:
time: 89.5 us; the launch traced here: 89.4 us
  Pallas kernels  86.7 us (97%)
  local copies, waits for them, and re-layouts  2.65 us (3%)
    pallas_call x1, Pallas kernels, on_device(): pl.pallas_call(kernel, out_shape=jax.ShapeDtypeStruct((ROWS, LEVD * COLS)...  86.7 us
    unnamed x1, local copies, waits for them, and re-layouts  2.65 us

profile of v2, /device:TPU:1, one launch (start us, length us, event | category | flops | bytes accessed | tf_op | source)
XLA Modules:
  0.0 89.4 jit_solution(16771293547105096479)
XLA Ops:
  0.0 86.7 %shard_map.91 = f32[96,4096]{1,0:T(8,128)} custom-call(bf16[96,4096]{1,0:T(8,128)(2,1)} %bitcast.8, bf16[8,616,384]{2,1,0:T(8,128)(2,1)} %jac_hbm.1, bf16[616,8192]{1,0:T(8,128)(2,1)} %dep_hbm.1, f32[8,8192]{1,0:T(8,128)} %pred_hbm.1, f32[8,616]{1,0:T(8,128)} %bitcast.10, f32[616]{0:T(1024)} %sigma_hbm.1, s32[8,616]{1,0:T(8,128)} %use_hbm.1, ...), custom_call_target="tpu_custom_call" | custom-call | tf_op jit(solution)/shard_map/pallas_call | solution.py:334
  86.7 2.7 %copy.11 = f32[3,32,4096]{2,1,0:T(8,128)} copy(f32[3,32,4096]{2,1,0:T(8,128)} %bitcast.7) | data formatting | bytes 3145728

commit v3 on v2

--- a/solution.py
+++ b/solution.py
@@ -24,6 +24,8 @@
 TILE = 1024
 TILES = 8
 OBS = TILE * TILES
+PARTS = 2
+DEEP = OBS // PARTS
 F32 = jnp.float32
 BF16 = jnp.bfloat16
 
@@ -91,22 +93,6 @@
         pl.semaphore_signal(barrier, inc=1, device_id=near(i), device_id_type=MESH)
     for i in range(1, COLD // 2):
         pl.semaphore_signal(barrier, inc=1, device_id=far(i), device_id_type=MESH)
-    loads[0].wait()
-    pl.semaphore_wait(barrier, 2 * LEVD - 1 + COLD // 2 - 1)
-
-    def list_copy(i):
-        other = lax.rem(lev + i, LEVD)
-        return pltpu.make_async_remote_copy(
-            src_ref=lists.at[lev], dst_ref=lists.at[lev], send_sem=list_send.at[i],
-            recv_sem=list_recv.at[i], device_id=(other, col), device_id_type=MESH,
-        )
-
-    for i in range(1, LEVD):
-        list_copy(i).start()
-    for i in range(1, 2 * LEVD):
-        pl.semaphore_signal(all_sem, inc=1, device_id=near(i), device_id_type=MESH)
-    loads[1].wait()
-
     def build_pick(owner):
         def build(k, carry):
             row = lists[owner, pl.ds(k, 1), :].astype(F32)
@@ -117,17 +103,32 @@
 
         lax.fori_loop(0, CAP, build, 0)
 
-    for i in range(LEVD):
-        owner = lax.rem(lev + (LEVD - i), LEVD)
-        if i:
-            list_copy(i).wait_recv()
-
+    def gather(owner):
         build_pick(owner)
         at = pl.multiple_of(owner * COLS, COLS)
         to = pl.multiple_of(owner * ROWS, 32)
         gath[pl.ds(to, ROWS), :] = jnp.dot(
             inc[:, pl.ds(at, COLS)], hot[:, pl.ds(at, SLOTS)], preferred_element_type=F32
         )
+
+    def list_copy(i):
+        other = lax.rem(lev + i, LEVD)
+        return pltpu.make_async_remote_copy(
+            src_ref=lists.at[lev], dst_ref=lists.at[lev], send_sem=list_send.at[i],
+            recv_sem=list_recv.at[i], device_id=(other, col), device_id_type=MESH,
+        )
+
+    loads[0].wait()
+    loads[1].wait()
+    gather(lev)
+    pl.semaphore_wait(barrier, 2 * LEVD - 1 + COLD // 2 - 1)
+    for i in range(1, LEVD):
+        list_copy(i).start()
+    for i in range(1, 2 * LEVD):
+        pl.semaphore_signal(all_sem, inc=1, device_id=near(i), device_id_type=MESH)
+    for i in range(1, LEVD):
+        list_copy(i).wait_recv()
+        gather(lax.rem(lev + (LEVD - i), LEVD))
     for i in range(1, LEVD):
         list_copy(i).wait_send()
     for k in range(CAP):
@@ -243,73 +244,84 @@
 
     lax.fori_loop(0, TILES, observe, 0)
 
-    def give_back(step, carry):
-        pair = lax.rem(lev // 2 + step // 2, 2)
-        half = lax.rem(col // 16 + step, 2)
-        acc[...] = jnp.zeros_like(acc)
+    plane = col // 8
+    offsets = (2, 1, 3, 0)
+
+    def push(step, i):
+        row = lax.rem(lev + i // 8, LEVD)
+        other = row * COLD + lax.rem(plane + offsets[step], 4) * 8 + lax.rem(col + i, 8)
+        for src, dst, send, receive in (
+            (rsend.at[other], rrecv.at[me], rsend_sem, rrecv_sem),
+            (units_out.at[step, row // 2], units_in.at[me], msend_sem, mrecv_sem),
+        ):
+            pltpu.make_async_remote_copy(
+                src_ref=src, dst_ref=dst, send_sem=send, recv_sem=receive,
+                device_id=peer_id(other), device_id_type=MESH,
+            ).start()
+
+    for step in range(4):
+        target = lax.rem(plane + offsets[step], 4)
 
         def add(t, inner):
-            at = pl.multiple_of(t * TILE, TILE)
-            left = adj[pl.ds(pair * 2, 2), :, :, pl.ds(at, TILE)].reshape(4 * ROWS, TILE)
+            if step:
+                for n in range(32 // PARTS):
+                    push(step - 1, t * (32 // PARTS) + n)
+            at = pl.multiple_of(t * DEEP, DEEP)
+            left = adj[:, :, :, pl.ds(at, DEEP)].reshape(8 * ROWS, DEEP)
             right = jnp.concatenate(
                 [
-                    hot[pl.ds(pl.multiple_of(owner * 256 + half * 128, 128), 128), pl.ds(at, TILE)]
+                    hot[pl.ds(pl.multiple_of(owner * 256 + target * 64, 64), 64), pl.ds(at, DEEP)]
                     for owner in range(LEVD)
                 ],
                 axis=0,
             )
-            acc[...] += lax.dot_general(
-                left, right, (((1,), (1,)), ((), ())), preferred_element_type=F32
-            )
+            more = lax.dot_general(left, right, (((1,), (1,)), ((), ())), preferred_element_type=F32)
+
+            acc[...] += more
             return inner
 
-        lax.fori_loop(0, TILES, add, 0)
-        for h in range(2):
-            total = acc[h * 192 : h * 192 + ROWS, :] + acc[h * 192 + ROWS : (h + 1) * 192, :]
-            tall = jnp.concatenate([total[:, o * 128 : (o + 1) * 128] for o in range(LEVD)], axis=0)
+        acc[...] = jnp.zeros_like(acc)
+        lax.fori_loop(0, PARTS, add, 0)
+        for pair in range(2):
+            parts = []
+            for h in (2 * pair, 2 * pair + 1):
+                total = acc[h * 192 : h * 192 + ROWS, :] + acc[h * 192 + ROWS : (h + 1) * 192, :]
+                parts.append(
+                    jnp.concatenate([total[:, o * 64 : (o + 1) * 64] for o in range(LEVD)], axis=0)
+                )
+            tall = jnp.concatenate(parts, axis=1)
             unit = jnp.max(jnp.abs(tall), axis=0, keepdims=True) * (1.0 / 32767.0)
             per = jnp.where(unit > 1e-37, 1.0 / unit, 0.0)
-            units_out[pair * 2 + h, half] = unit
+            units_out[step, pair] = unit
             code = jnp.round(tall * per).T.astype(jnp.int32).astype(jnp.int16)
-            rsend[pl.ds((pair * 2 + h) * COLD + half * 16, 16)] = code.reshape(16, CAP, PROF)
-
-        def push(i, inner):
-            other = (pair * 2 + i // 16) * COLD + half * 16 + lax.rem(i + col, 16)
-            moves = (
-                (rsend.at[other], rrecv.at[me], rsend_sem, rrecv_sem),
-                (units_out.at[pair * 2 + i // 16, half], units_in.at[me], msend_sem, mrecv_sem),
-            )
-
-            @pl.when(other != me)
-            def _():
-                for src, dst, send, receive in moves:
-                    pltpu.make_async_remote_copy(
-                        src_ref=src, dst_ref=dst, send_sem=send, recv_sem=receive,
-                        device_id=peer_id(other), device_id_type=MESH,
-                    ).start()
-
-            @pl.when(other == me)
-            def _():
-                for n, (src, dst, send, receive) in enumerate(moves):
-                    pltpu.make_async_copy(src, dst, own_sem.at[1 + n]).start()
-
-            return inner
-
-        lax.fori_loop(0, 32, push, 0)
+            for h in range(2):
+                rsend[pl.ds((2 * pair + h) * COLD + target * 8, 8)] = code[h * 64 : (h + 1) * 64, :].reshape(
+                    8, CAP, PROF
+                )
+
+    kept = (
+        pltpu.make_async_copy(rsend.at[me], rrecv.at[me], own_sem.at[1]),
+        pltpu.make_async_copy(units_out.at[3, lev // 2], units_in.at[me], own_sem.at[2]),
+    )
+
+    def last(i, carry):
+        push(3, i)
         return carry
 
-    lax.fori_loop(0, 4, give_back, 0)
+    lax.fori_loop(1, 32, last, 0)
+    for copy in kept:
+        copy.start()
     for owner in range(LEVD):
         build_pick(owner)
-    pltpu.make_async_copy(rsend.at[me], rrecv.at[me], own_sem.at[1]).wait()
-    pltpu.make_async_copy(units_in.at[me], units_in.at[me], own_sem.at[2]).wait()
+    for copy in kept:
+        copy.wait()
     most = pl.ds(0, NDEV - 1)
     for sem in (msend_sem, mrecv_sem):
         pltpu.make_async_copy(units_in.at[most], units_in.at[most], sem).wait()
     pltpu.make_async_copy(rsend.at[most], rsend.at[most], rsend_sem).wait()
     pltpu.make_async_copy(rrecv.at[most], rrecv.at[most], rrecv_sem).wait()
     square[...] = units_in[:, 0, :].T
-    units = square[pl.ds(pl.multiple_of(lax.rem(col, 16) * CAP, CAP), CAP), :]
+    units = square[pl.ds(pl.multiple_of(lax.rem(lev, 2) * 64 + lax.rem(col, 8) * CAP, CAP), CAP), :]
     for m in range(NF):
         rows8[m] = rrecv[:, :, m * 128 : (m + 1) * 128].astype(jnp.int32).astype(F32).reshape(SLOTS, 128)
 
@@ -358,10 +370,10 @@
             pltpu.VMEM((128, 128), F32),
             pltpu.VMEM((CPAD, TILE), BF16),
             pltpu.VMEM((LEVD, 2, ROWS, OBS), BF16),
-            pltpu.VMEM((4 * ROWS, 512), F32),
+            pltpu.VMEM((8 * ROWS, 256), F32),
             pltpu.VMEM((NDEV, CAP, PROF), jnp.int16),
             pltpu.VMEM((NDEV, CAP, PROF), jnp.int16),
-            pltpu.VMEM((LEVD, 2, 1, 128), F32),
+            pltpu.VMEM((4, 2, 1, 128), F32),
             pltpu.VMEM((NDEV, 1, 128), F32),
             pltpu.VMEM((NF, SLOTS, 128), F32),
             pltpu.VMEM((LEVD, 2 * ROWS, SLOTS), BF16),

time: 89.5 us -> 82 us (0.916)
  Pallas kernels: 86.7 us -> 79.2 us
    pallas_call x1, Pallas kernels: 86.7 us -> 79.2 us  [on_device(): pl.pallas_call(kernel, out_shape=jax.ShapeDtypeStruct((ROWS, LEVD * COLS)...]
where the time goes in v3:
time: 82 us; the launch traced here: 81.9 us
  Pallas kernels  79.2 us (97%)
  local copies, waits for them, and re-layouts  2.65 us (3%)
    pallas_call x1, Pallas kernels, on_device(): pl.pallas_call(kernel, out_shape=jax.ShapeDtypeStruct((ROWS, LEVD * COLS)...  79.2 us
    unnamed x1, local copies, waits for them, and re-layouts  2.65 us

profile of v3, /device:TPU:1, one launch (start us, length us, event | category | flops | bytes accessed | tf_op | source)
XLA Modules:
  0.0 81.9 jit_solution(6181939901836008857)
XLA Ops:
  0.0 79.2 %shard_map.91 = f32[96,4096]{1,0:T(8,128)} custom-call(bf16[96,4096]{1,0:T(8,128)(2,1)} %bitcast.8, bf16[8,616,384]{2,1,0:T(8,128)(2,1)} %jac_hbm.1, bf16[616,8192]{1,0:T(8,128)(2,1)} %dep_hbm.1, f32[8,8192]{1,0:T(8,128)} %pred_hbm.1, f32[8,616]{1,0:T(8,128)} %bitcast.10, f32[616]{0:T(1024)} %sigma_hbm.1, s32[8,616]{1,0:T(8,128)} %use_hbm.1, ...), custom_call_target="tpu_custom_call" | custom-call | tf_op jit(solution)/shard_map/pallas_call | solution.py:346
  79.2 2.7 %copy.11 = f32[3,32,4096]{2,1,0:T(8,128)} copy(f32[3,32,4096]{2,1,0:T(8,128)} %bitcast.7) | data formatting | bytes 3145728

commit v4 on v3

--- a/solution.py
+++ b/solution.py
@@ -222,15 +222,15 @@
         xaug[PROF : PROF + 128, :] = paug[:, pl.ds(at, TILE)]
         dep_load(t).wait()
         half = lax.rem(t, 2)
-        for n in range(TILE // 256):
-            lanes = slice(n * 256, (n + 1) * 256)
+        for n in range(TILE // 512):
+            lanes = slice(n * 512, (n + 1) * 512)
             tangent = jnp.dot(jaug[t], xaug[:, lanes], preferred_element_type=F32)
             factor = scale[t, 0:CHAN, :]
             residual = tangent - dep[half, :, lanes].astype(F32)
-            forcing[0:CHAN, lanes] = (jnp.concatenate([factor, factor], axis=1) * residual).astype(BF16)
-        for n in range(TILE // 256):
-            lanes = slice(n * 256, (n + 1) * 256)
-            to = pl.multiple_of(at + n * 256, 256)
+            forcing[0:CHAN, lanes] = (jnp.concatenate([factor] * 4, axis=1) * residual).astype(BF16)
+        for n in range(TILE // 512):
+            lanes = slice(n * 512, (n + 1) * 512)
+            to = pl.multiple_of(at + n * 512, 512)
             value = jnp.dot(jt[t], forcing[:, lanes], preferred_element_type=F32)
             first = value.astype(BF16)
             second = (value - first.astype(F32)).astype(BF16)
@@ -238,8 +238,8 @@
                 for field in range(NF):
                     rows = slice(field * 128 + h * SLAB, field * 128 + (h + 1) * SLAB)
                     put = slice(field * SLAB, (field + 1) * SLAB)
-                    adj[h, 0, put, pl.ds(to, 256)] = first[rows, :]
-                    adj[h, 1, put, pl.ds(to, 256)] = second[rows, :]
+                    adj[h, 0, put, pl.ds(to, 512)] = first[rows, :]
+                    adj[h, 1, put, pl.ds(to, 512)] = second[rows, :]
         return carry
 
     lax.fori_loop(0, TILES, observe, 0)

time: 82 us -> 81 us (0.988)
  Pallas kernels: 79.2 us -> 78.2 us
    pallas_call x1, Pallas kernels: 79.2 us -> 78.2 us  [on_device(): pl.pallas_call(kernel, out_shape=jax.ShapeDtypeStruct((ROWS, LEVD * COLS)...]
where the time goes in v4:
time: 81 us; the launch traced here: 80.9 us
  Pallas kernels  78.2 us (97%)
  local copies, waits for them, and re-layouts  2.65 us (3%)
    pallas_call x1, Pallas kernels, on_device(): pl.pallas_call(kernel, out_shape=jax.ShapeDtypeStruct((ROWS, LEVD * COLS)...  78.2 us
    unnamed x1, local copies, waits for them, and re-layouts  2.65 us

profile of v4, /device:TPU:1, one launch (start us, length us, event | category | flops | bytes accessed | tf_op | source)
XLA Modules:
  0.0 80.9 jit_solution(3627374880421422378)
XLA Ops:
  0.0 78.2 %shard_map.91 = f32[96,4096]{1,0:T(8,128)} custom-call(bf16[96,4096]{1,0:T(8,128)(2,1)} %bitcast.8, bf16[8,616,384]{2,1,0:T(8,128)(2,1)} %jac_hbm.1, bf16[616,8192]{1,0:T(8,128)(2,1)} %dep_hbm.1, f32[8,8192]{1,0:T(8,128)} %pred_hbm.1, f32[8,616]{1,0:T(8,128)} %bitcast.10, f32[616]{0:T(1024)} %sigma_hbm.1, s32[8,616]{1,0:T(8,128)} %use_hbm.1, ...), custom_call_target="tpu_custom_call" | custom-call | tf_op jit(solution)/shard_map/pallas_call | solution.py:346
  78.2 2.7 %copy.11 = f32[3,32,4096]{2,1,0:T(8,128)} copy(f32[3,32,4096]{2,1,0:T(8,128)} %bitcast.7) | data formatting | bytes 3145728
